TPU v7x, 128 devices: a whole 4x4x4 slice. The times are simulated.
128 devices in a mesh: grp: 16 (over x, y_lo, core), dev: 8 (over y_hi, z).
Axes of the slice: x: 4, y: 4 (y_hi: 2, y_lo: 2; y = y_hi * 2 + y_lo), z: 4, core: 2. Of those that a mesh axis runs over, the one named last changes fastest.
Arguments:
- tile_patches: bfloat16 [12288, 588], P(('grp', 'dev')), may hold values from -6 to 6
- w_patch: bfloat16 [588, 1536], replicated, may hold values from -0.25 to 0.25
- w_tqkv: bfloat16 [3, 1536, 1536], P(None, None, 'dev'), may hold values from -6 to 6
- w_to: bfloat16 [1536, 1536], P('dev'), may hold values from -0.15625 to 0.15625
- w_gu: bfloat16 [2, 1536, 4096], P(None, None, 'dev'), may hold values from -0.15625 to 0.15625
- w_down: bfloat16 [4096, 1536], P('dev'), may hold values from -0.09375 to 0.09375
- tile_gain: float32 [3, 1536], replicated, may hold values from 0.1 to 1.9
- w_in: bfloat16 [1536, 768], replicated, may hold values from -0.15625 to 0.15625
- slide_tokens: bfloat16 [262144, 768], P(('grp', 'dev')), may hold values from -6 to 6
- slide_gain: float32 [768], replicated, may hold values from 0.1 to 1.9
- w_sqkv: bfloat16 [3, 768, 768], replicated, may hold values from -6 to 6
- w_so: bfloat16 [768, 768], replicated, may hold values from -1.75 to 1.75
- pattern_of_group: int32 [4], replicated, may hold values from 0 to 3, each once
- new_positions: int32 [48], replicated, may hold values from 0 to 262143, as said below
Outputs:
- tile_embed: bfloat16 [48, 768], P('grp')
- slide_out: bfloat16 [262144, 768], P(('grp', 'dev'))
Inputs may be any that keep to these rules, and one draw needn't show every extreme that they name: `pattern_of_group`: each of the four patterns is used by exactly one head group. `new_positions`: distinct positions.
All inputs are finite; a program needn't handle non-finite values.
Results may differ from a plain program's by a relative error of at most 0.025.
Values may be sent and summed in bfloat16 or wider, within the bound.
A program may use at most 256 MiB of HBM per device.

v0:
```python
import functools

import jax
import jax.numpy as jnp
from jax import lax
from jax.experimental import pallas as pl
from jax.experimental.pallas import tpu as pltpu
from jax.sharding import PartitionSpec as P

MESH = pl.DeviceIdType.MESH
BF16 = jnp.bfloat16
F32 = jnp.float32

TW = 1536
TH = 64
TP = 256
HB = 192
FB = 512
SW = 768
GW = 192
SH = 48
ROWS = 2048
DIL = (1, 8, 32, 128)
LOG2E = 1.4426950408889634
HIDE = -1e30
KEYS_AT, HALF_AT, FEED_AT, EMBED_AT = 6, 10, 12, 14
SCALE = LOG2E * SH**-0.5


def dot(a, b):
    return jnp.dot(a, b, preferred_element_type=F32)


def dot_nt(a, b):
    return lax.dot_general(a, b, (((1,), (1,)), ((), ())), preferred_element_type=F32)


def norm(v, gain):
    center = v - jnp.mean(v, axis=-1, keepdims=True)
    spread = jnp.mean(center * center, axis=-1, keepdims=True)
    return center * lax.rsqrt(spread + 1e-06) * gain


def head_of(shape):
    return (lax.broadcasted_iota(jnp.int32, shape, 1) % GW) // SH


def attend(q, keys, values):
    s = dot_nt(q, keys)
    m = jnp.max(s, axis=-1, keepdims=True)
    e = jnp.exp2((s - m) * SCALE).astype(BF16)
    return m, e, dot(e, values)


def with_ones(vt):
    tail = lax.broadcasted_iota(jnp.int32, (16, vt.shape[1]), 0) == 0
    tail = jnp.where(tail, 1.0, 0.0)
    pieces = []
    for j in range(4):
        pieces += [vt[j * SH : (j + 1) * SH, :], tail]
    return jnp.concatenate(pieces, axis=0).astype(BF16)


def only_head(j, rows, bias=False, shift=False):
    lane = lax.broadcasted_iota(jnp.int32, (rows, 256), 1)
    mine = jnp.logical_and(lane >= j * SH, lane < (j + 1) * SH)
    if bias:
        mine = jnp.logical_or(mine, lane == GW)
    if shift:
        mine = jnp.logical_or(mine, lane == GW + 1 + j)
    return mine


def encoder_kernel(
    patches,
    w_patch,
    w_tqkv,
    w_to,
    w_gu,
    w_down,
    w_in,
    tokens,
    w_sqkv,
    tgain,
    sgain,
    positions,
    pattern,
    qk0_out,
    vt0_out,
    near,
    stats,
    q1_out,
    q2_out,
    q3_out,
    kv1,
    kv2,
    kv3,
    em,
    new_out,
    patches_s,
    w_patch_s,
    w_tqkv_s,
    wto_s,
    w_gu_s,
    w_down_s,
    w_in_s,
    tok_s,
    w_raw,
    w_slide_s,
    hs,
    qk0_s,
    vt0_s,
    kvc1,
    kvc2,
    kvc3,
    x0_s,
    att_s,
    pp_s,
    largest,
    x_sum_s,
    load_sem,
    out_sem,
    own_sem,
    send_sem,
    recv_sem,
    att_send,
    att_recv,
):
    grp = lax.axis_index("grp")
    dev = lax.axis_index("dev")
    core = grp % 2
    plane = grp // 4
    chip = (grp // 2) * 8 + dev
    local16 = (grp // 2) % 2 * 8 + dev
    sibling = (grp // 2) * 2 + (1 - core)

    z = dev % 4
    side = (grp // 2) % 2 * 2 + dev // 4

    def peer8(i):
        return (grp, (dev + i) % 8)

    def peer_z(i):
        return (grp, dev // 4 * 4 + (z + i) % 4)

    def peer_y(i):
        to = (side + i) % 4
        return (plane * 4 + to // 2 * 2 + core, to % 2 * 4 + z)

    def peer_x(i):
        return ((plane + i) % 4 * 4 + grp % 4, dev)

    def peer_grp(i):
        return ((grp + i) % 16, dev)

    def load(src, dst, at):
        copy = pltpu.make_async_copy(src, dst, load_sem.at[at])
        copy.start()
        return copy

    ld_tok = load(tokens, tok_s, 0)
    ld_raw = load(w_sqkv, w_raw, 1)
    ld_patch = load(w_patch, w_patch_s, 2)
    ld_tqkv = load(w_tqkv, w_tqkv_s, 3)
    ld_gu = load(w_gu, w_gu_s, 4)
    ld_down = load(w_down, w_down_s, 5)
    ld_in = load(w_in, w_in_s, 6)

    my_patch = pl.ds(pl.multiple_of(dev * 96, 32), 96)
    half_row = pl.multiple_of(core * 96, 32)
    my_half = pl.ds(pl.multiple_of(dev * HB + core * 96, 32), 96)
    quarter = pl.ds(pl.multiple_of(plane * 384, 128), 384)
    my_shard = pl.ds(pl.multiple_of(dev * HB, 64), HB)

    barrier = pltpu.get_barrier_semaphore()

    @pl.loop(1, 8)
    def _(i):
        pl.semaphore_signal(barrier, inc=1, device_id=peer8(i), device_id_type=MESH)

    @pl.loop(1, 16)
    def _(i):
        pl.semaphore_signal(barrier, inc=1, device_id=peer_grp(i), device_id_type=MESH)

    across = (plane * 4 + (1 - side // 2) * 2 + core, (dev + 4) % 8)
    pl.semaphore_signal(barrier, inc=1, device_id=across, device_id_type=MESH)
    pl.semaphore_wait(barrier, 23)

    own_patch = pltpu.make_async_copy(patches, patches_s.at[my_patch], own_sem.at[0])
    own_patch.start()
    own_wto = pltpu.make_async_copy(w_to, wto_s.at[my_shard], own_sem.at[1])
    own_wto.start()

    def push(src, dst, at, to):
        pltpu.make_async_remote_copy(
            src_ref=src,
            dst_ref=dst,
            send_sem=send_sem.at[at],
            recv_sem=recv_sem.at[at],
            device_id=to,
            device_id_type=MESH,
        ).start()

    def landed(ref, sem):
        pltpu.make_async_copy(ref, ref, sem).wait()

    @pl.loop(1, 8)
    def _(i):
        push(patches, patches_s.at[my_patch], 0, peer8(i))

    @pl.loop(1, 8)
    def _(i):
        push(w_to.at[pl.ds(half_row, 96), quarter], wto_s.at[my_half, quarter], 1, peer8(i))

    ld_raw.wait()
    group = [
        sum(jnp.where(pattern[g] == p, g, 0) for g in range(4)) for p in range(4)
    ]

    @pl.loop(0, 3)
    def _(c):
        at = pl.ds(pl.multiple_of(c * 256, 256), 256)

        def part(index, p):
            pair = jnp.where(group[p] >= 2, w_raw[index, at, 384:], w_raw[index, at, :384])
            return jnp.where(group[p] % 2 == 1, pair[:, GW:], pair[:, :GW])

        for index in range(3):
            w_slide_s[0, at, index * 256 : (index + 1) * 256] = jnp.concatenate(
                [part(index, 0), jnp.zeros((256, 64), BF16)], axis=1
            )
        for p in range(1, 4):
            w_slide_s[p, at, :384] = jnp.concatenate([part(2, p), part(1, p)], axis=1)
            w_slide_s[p, at, 384:] = jnp.concatenate(
                [jnp.zeros((256, GW), BF16), part(0, p)], axis=1
            )

    lane128 = lax.broadcasted_iota(jnp.int32, (1, 128), 1)
    places = lax.fori_loop(
        0,
        48,
        lambda n, held: jnp.where(lane128 == n, positions[n], held),
        jnp.full((1, 128), -1, jnp.int32),
    )
    ld_tok.wait()
    first = (grp * 8 + dev) * ROWS
    source = lax.broadcasted_iota(jnp.int32, (256, 256), 0)
    target = lax.broadcasted_iota(jnp.int32, (256, 256), 1)
    to_lane = jnp.logical_and(source < GW, target == GW + 1 + source // SH)
    to_lane = jnp.where(to_lane, 1.0, 0.0).astype(BF16)
    largest[...] = jnp.zeros_like(largest)

    @pl.loop(0, 8)
    def _(c):
        at = pl.ds(pl.multiple_of(c * 256, 256), 256)
        h = norm(tok_s[at, :].astype(F32), sgain[...].reshape(1, SW))
        for b in range(6):
            hs[b, at, :] = h[:, b * 128 : (b + 1) * 128]
        y = dot(h.astype(BF16), w_slide_s[0])
        row = lax.broadcasted_iota(jnp.int32, (256, 128), 0) + (first + c * 256)
        stale = jnp.max(jnp.where(row == places, 1.0, 0.0), axis=1, keepdims=True)
        column = lax.broadcasted_iota(jnp.int32, (256, 256), 1)
        q = y[:, 0:256].astype(BF16)
        k = y[:, 256:512].astype(BF16)
        q_size = jnp.sqrt(dot((q.astype(F32) * q.astype(F32)).astype(BF16), to_lane)) * 1.02
        k_size = dot((k.astype(F32) * k.astype(F32)).astype(BF16), to_lane)
        largest[...] = jnp.maximum(largest[...], jnp.max(k_size, axis=0, keepdims=True))
        q = jnp.where(column == GW, 1.0, q.astype(F32) - q_size)
        qk0_s[at, 0:256] = q.astype(BF16)
        qk0_s[at, 256:512] = jnp.where(column == GW, stale * HIDE, k.astype(F32)).astype(BF16)
        vt0_s[:, at] = with_ones(y[:, 512 : 512 + GW].T)

    bound = (jnp.sqrt(largest[...]) * 1.02).astype(BF16)

    @pl.loop(0, 8)
    def _(c):
        at = pl.ds(pl.multiple_of(c * 256, 256), 256)
        k = qk0_s[at, 256:512]
        qk0_s[at, 256:512] = jnp.where(target > GW, bound.astype(F32), k.astype(F32)).astype(BF16)

    out0 = pltpu.make_async_copy(qk0_s, qk0_out, out_sem.at[0])
    out0.start()
    out1 = pltpu.make_async_copy(vt0_s, vt0_out, out_sem.at[1])
    out1.start()

    own_patch.wait()
    landed(patches_s.at[pl.ds(0, 672)], recv_sem.at[0])
    ld_patch.wait()
    ld_tqkv.wait()

    lanes = lax.broadcasted_iota(jnp.int32, (TP, HB), 1) // TH

    @pl.loop(0, 3)
    def _(t):
        at = pl.ds(pl.multiple_of(t * TP, TP), TP)
        @pl.when(t == 1)
        def _():
            own_wto.wait()
            landed(wto_s.at[pl.ds(0, 672), quarter], recv_sem.at[1])

            @pl.loop(1, 8)
            def _(i):
                half = pl.ds(pl.multiple_of(((dev + i) % 8) * HB + core * 96, 32), 96)

                @pl.loop(1, 4)
                def _(step):
                    push(wto_s.at[half, quarter], wto_s.at[half, quarter], 10, peer_x(step))

        x0 = dot(patches_s[at, :], w_patch_s[...]).astype(BF16)
        x0_s[at, :] = x0
        h1 = norm(x0.astype(F32), tgain[0:1, :]).astype(BF16)
        q = dot_nt(h1, w_tqkv_s[0]).astype(BF16)
        k = dot_nt(h1, w_tqkv_s[1]).astype(BF16)
        vt = dot_nt(w_tqkv_s[2], h1).astype(BF16)
        for h in range(3):
            s = dot_nt(jnp.where(lanes == h, q, jnp.zeros_like(q)), k) * (TH**-0.5)
            e = jnp.exp(s - jnp.max(s, axis=-1, keepdims=True))
            probs = (e / jnp.sum(e, axis=-1, keepdims=True)).astype(BF16)
            o = dot_nt(vt[h * TH : (h + 1) * TH, :], probs)
            rows = pl.ds(pl.multiple_of(dev * HB + h * TH, 64), TH)
            att_s[t, rows, :] = o.astype(BF16)

        @pl.loop(1, 8)
        def _(i):
            pltpu.make_async_remote_copy(
                src_ref=att_s.at[t, my_shard],
                dst_ref=att_s.at[t, my_shard],
                send_sem=att_send.at[t],
                recv_sem=att_recv.at[t],
                device_id=peer8(i),
                device_id_type=MESH,
            ).start()

    for p, kvc, q_out in ((1, kvc1, q1_out), (2, kvc2, q2_out), (3, kvc3, q3_out)):
        r = DIL[p]
        n = ROWS // r
        picked = jnp.concatenate(
            [
                jnp.concatenate([hs[b, pl.ds(j, n, stride=r), :] for b in range(6)], axis=1)
                for j in range(4)
            ],
            axis=0,
        ).astype(BF16)
        y = dot(picked, w_slide_s[p])
        head = head_of((n, SW))
        mine = jnp.zeros((n, SW), F32)
        for j in range(4):
            mine = jnp.where(head == j, y[j * n : (j + 1) * n, :], mine)
        kvc[...] = mine[:, :384].astype(BF16)
        q_out[...] = mine[:, 384:].astype(BF16)

    at1 = pl.ds(pl.multiple_of(dev * 256, 256), 256)
    at1_y = pl.ds(pl.multiple_of((dev + 4) % 8 * 256, 256), 256)
    at2 = pl.ds(pl.multiple_of((core * 16 + local16) * 64, 64), 64)
    at2_z = pl.ds(pl.multiple_of((core * 16 + local16 // 4 * 4) * 64, 256), 256)
    at3 = pl.ds(pl.multiple_of((core * 64 + chip) * 16, 16), 16)
    at3_z = pl.ds(pl.multiple_of((core * 64 + chip // 4 * 4) * 16, 64), 64)
    at3_y = pl.ds(pl.multiple_of((core * 64 + chip // 16 * 16) * 16, 256), 256)
    own1 = pltpu.make_async_copy(kvc1, kv1.at[at1], own_sem.at[2])
    own2 = pltpu.make_async_copy(kvc2, kv2.at[at2], own_sem.at[3])
    own3 = pltpu.make_async_copy(kvc3, kv3.at[at3], own_sem.at[4])
    own1.start()
    own2.start()
    own3.start()

    eight = lax.broadcasted_iota(jnp.int32, (8, 1), 0)
    half3 = pl.ds(pl.multiple_of(core * 1024, 1024), 1024)

    def feed(t, sums):
        x_sum, h_sum = sums
        at = pl.ds(pl.multiple_of(t * TP, TP), TP)
        landed(att_s.at[t, pl.ds(0, 7 * HB)], att_recv.at[t])
        att = att_s[t].T
        x1 = (x0_s[at, :].astype(F32) + dot(att, wto_s[...])).astype(BF16).astype(F32)
        h2 = norm(x1, tgain[1:2, :]).astype(BF16)
        gate = dot(h2, w_gu_s[0])
        up = dot(h2, w_gu_s[1])
        hidden = (jax.nn.silu(gate) * up).astype(BF16).astype(F32)
        x_sum = x_sum + jnp.where(eight == t, jnp.sum(x1, axis=0, keepdims=True), 0.0)
        h_sum = h_sum + jnp.where(eight == t, jnp.sum(hidden, axis=0, keepdims=True), 0.0)
        return x_sum, h_sum

    @pl.loop(0, 16)
    def _(u):
        j = u % 4
        at = pl.ds(pl.multiple_of(u // 4 * 512, 512), 512)
        q = qk0_s[at, 0:256]
        q = jnp.where(only_head(j, 512, True, True), q, jnp.zeros_like(q))
        e = jnp.exp2(dot_nt(qk0_s[:, 256:512], q) * SCALE).astype(BF16)
        o = dot(vt0_s[pl.ds(pl.multiple_of(j * 64, 64), 64), :], e)
        count = o[SH : SH + 1, :]
        near[pl.ds(pl.multiple_of(j * SH, 16), SH), at] = (o[:SH, :] / count).astype(BF16)
        lane = lax.broadcasted_iota(jnp.int32, (8, 256), 1)
        limit = jnp.where(lane == GW + 1 + j, -bound.astype(F32), 0.0).astype(BF16)
        stats[j, :, at] = dot_nt(limit, q)
        stats[4 + j, :, at] = jnp.broadcast_to(count, (8, 512))

        @pl.when(u == KEYS_AT)
        def _():
            push(kvc1, kv1.at[at1], 13, (grp, (dev + 4) % 8))

            @pl.loop(1, 4)
            def _(i):
                push(kvc3, kv3.at[at3], 2, peer_z(i))
                push(kvc2, kv2.at[at2], 11, peer_z(i))
                push(kvc1, kv1.at[at1], 14, peer_z(i))

        @pl.when(u == HALF_AT)
        def _():
            landed(wto_s.at[pl.ds(0, 672), pl.ds(0, 1152)], recv_sem.at[10])

            @pl.loop(1, 8)
            def _(i):
                half = pl.ds(pl.multiple_of(((dev + i) % 8) * HB + core * 96, 32), 96)
                push(wto_s.at[half], wto_s.at[half], 5, (sibling, dev))

        @pl.when(u == FEED_AT)
        def _():
            own3.wait()
            landed(kv3.at[pl.ds(0, 3 * 16)], recv_sem.at[2])
            own2.wait()
            landed(kv2.at[pl.ds(0, 3 * 64)], recv_sem.at[11])
            landed(kv1.at[at1_y], recv_sem.at[13])

            @pl.loop(1, 4)
            def _(i):
                push(kv3.at[at3_z], kv3.at[at3_z], 3, peer_y(i))
                push(kv2.at[at2_z], kv2.at[at2_z], 12, peer_y(i))
                push(kv1.at[at1_y], kv1.at[at1_y], 14, peer_z(i))

            landed(wto_s.at[pl.ds(0, 672)], recv_sem.at[5])
            ld_gu.wait()
            x_sum, h_sum = lax.fori_loop(
                0, 3, feed, (jnp.zeros((8, TW), F32), jnp.zeros((8, FB), F32))
            )
            x_sum_s[...] = x_sum
            ld_down.wait()
            h_mean = h_sum * (1.0 / TP)
            coarse = h_mean.astype(BF16)
            fine = (h_mean - coarse.astype(F32)).astype(BF16)
            both = jnp.concatenate([coarse.astype(F32), fine.astype(F32)], axis=0).astype(BF16)
            part = dot(both, w_down_s[...])
            pp_s[dev] = part[0:8] + part[8:16]

            @pl.loop(1, 8)
            def _(i):
                push(pp_s.at[dev], pp_s.at[dev], 6, peer8(i))

            landed(kv3.at[pl.ds(0, 3 * 64)], recv_sem.at[3])

            @pl.loop(1, 4)
            def _(i):
                push(kv3.at[at3_y], kv3.at[at3_y], 4, peer_x(i))

        @pl.when(u == EMBED_AT)
        def _():
            ld_in.wait()
            landed(pp_s.at[pl.ds(0, 7)], recv_sem.at[6])
            pooled = x_sum_s[...] * (1.0 / TP) + jnp.sum(pp_s[...], axis=0)
            normed = norm(pooled, tgain[2:3, :]).astype(BF16)
            em[grp] = dot(normed, w_in_s[...]).astype(BF16).astype(F32)

            @pl.loop(1, 16)
            def _(i):
                push(em.at[grp], em.at[grp], 7, peer_grp(i))

            landed(kv2.at[pl.ds(0, 3 * 256)], recv_sem.at[12])
            push(kv2.at[half3], kv2.at[half3], 9, (sibling, dev))

    landed(kv3.at[pl.ds(0, 3 * 256)], recv_sem.at[4])
    push(kv3.at[half3], kv3.at[half3], 8, (sibling, dev))
    landed(em.at[pl.ds(0, 15)], recv_sem.at[7])
    tile = lax.broadcasted_iota(jnp.int32, (48, 128), 0)
    slot = lax.broadcasted_iota(jnp.int32, (48, 128), 1)
    gather = jnp.where(slot == tile // 3 * 8 + tile % 3, 1.0, 0.0).astype(BF16)
    fresh = dot(gather, em[...].reshape(128, SW).astype(BF16))
    fresh = norm(fresh, sgain[...].reshape(1, SW)).astype(BF16)
    for p in range(4):
        new_out[:, p * SW : (p + 1) * SW] = dot(fresh, w_slide_s[p])

    own1.wait()
    landed(kv1.at[pl.ds(0, 6 * 256)], recv_sem.at[14])
    landed(kv3.at[half3], recv_sem.at[8])
    landed(kv2.at[half3], recv_sem.at[9])
    out0.wait()
    out1.wait()

    landed(patches_s.at[pl.ds(0, 672)], send_sem.at[0])
    landed(wto_s.at[pl.ds(0, 672), quarter], send_sem.at[1])
    landed(wto_s.at[pl.ds(0, 672), pl.ds(0, 1152)], send_sem.at[10])
    landed(kv3.at[pl.ds(0, 3 * 16)], send_sem.at[2])
    landed(kv3.at[pl.ds(0, 3 * 64)], send_sem.at[3])
    landed(kv3.at[pl.ds(0, 3 * 256)], send_sem.at[4])
    landed(kv2.at[pl.ds(0, 3 * 64)], send_sem.at[11])
    landed(kv2.at[pl.ds(0, 3 * 256)], send_sem.at[12])
    landed(kv1.at[at1_y], send_sem.at[13])
    landed(kv1.at[pl.ds(0, 6 * 256)], send_sem.at[14])
    landed(wto_s.at[pl.ds(0, 672)], send_sem.at[5])
    landed(pp_s.at[pl.ds(0, 7)], send_sem.at[6])
    landed(em.at[pl.ds(0, 15)], send_sem.at[7])
    landed(kv3.at[half3], send_sem.at[8])
    landed(kv2.at[half3], send_sem.at[9])

    @pl.loop(0, 3)
    def _(t):
        landed(att_s.at[t, pl.ds(0, 7 * HB)], att_send.at[t])


def run_encoder(*args):
    hbm = pl.BlockSpec(memory_space=pl.ANY)
    vmem = pl.BlockSpec(memory_space=pltpu.VMEM)
    shape = jax.ShapeDtypeStruct
    return pl.pallas_call(
        encoder_kernel,
        out_shape=(
            shape((ROWS, 512), BF16),
            shape((256, ROWS), BF16),
            shape((GW, ROWS), BF16),
            shape((8, 8, ROWS), F32),
            shape((256, 384), BF16),
            shape((64, 384), BF16),
            shape((16, 384), BF16),
            shape((2048, 384), BF16),
            shape((2048, 384), BF16),
            shape((2048, 384), BF16),
            shape((16, 8, SW), F32),
            shape((48, 4 * SW), F32),
        ),
        in_specs=[hbm] * 9 + [vmem] * 2 + [pl.BlockSpec(memory_space=pltpu.SMEM)] * 2,
        out_specs=(hbm, hbm, vmem, vmem, vmem, vmem, vmem, hbm, hbm, hbm, vmem, vmem),
        scratch_shapes=[
            pltpu.VMEM((768, 588), BF16),
            pltpu.VMEM((588, TW), BF16),
            pltpu.VMEM((3, HB, TW), BF16),
            pltpu.VMEM((TW, TW), BF16),
            pltpu.VMEM((2, TW, FB), BF16),
            pltpu.VMEM((FB, TW), BF16),
            pltpu.VMEM((TW, SW), BF16),
            pltpu.VMEM((ROWS, SW), BF16),
            pltpu.VMEM((3, SW, SW), BF16),
            pltpu.VMEM((4, SW, SW), BF16),
            pltpu.VMEM((6, ROWS, 128), F32),
            pltpu.VMEM((ROWS, 512), BF16),
            pltpu.VMEM((256, ROWS), BF16),
            pltpu.VMEM((256, 384), BF16),
            pltpu.VMEM((64, 384), BF16),
            pltpu.VMEM((16, 384), BF16),
            pltpu.VMEM((768, TW), BF16),
            pltpu.VMEM((3, TW, TP), BF16),
            pltpu.VMEM((8, 8, TW), F32),
            pltpu.VMEM((1, 256), F32),
            pltpu.VMEM((8, TW), F32),
            pltpu.SemaphoreType.DMA((7,)),
            pltpu.SemaphoreType.DMA((2,)),
            pltpu.SemaphoreType.DMA((5,)),
            pltpu.SemaphoreType.DMA((15,)),
            pltpu.SemaphoreType.DMA((15,)),
            pltpu.SemaphoreType.DMA((3,)),
            pltpu.SemaphoreType.DMA((3,)),
        ],
        compiler_params=pltpu.CompilerParams(
            collective_id=0, has_side_effects=True, vmem_limit_bytes=60 * 1024 * 1024
        ),
        name="encode",
    )(*args)


def slide_kernel(
    positions,
    pattern,
    qk0,
    vt0,
    near,
    stats,
    q1,
    q2,
    q3,
    kv1,
    kv2,
    kv3,
    tokens,
    new,
    em,
    w_so,
    out,
    embed_out,
    qk0_s,
    vt0_s,
    near_s,
    stats_s,
    q1_s,
    q2_s,
    q3_s,
    kv1_s,
    kv2_s,
    kv3_s,
    tok_s,
    far_s,
    wso_s,
    sem,
):
    step = pl.program_id(0)
    place = lax.axis_index("grp") * 8 + lax.axis_index("dev")

    def weights(p):
        group = sum(jnp.where(pattern[g] == p, g, 0) for g in range(4))
        return w_so[pl.ds(pl.multiple_of(group * GW, 64), GW), :]

    @pl.when(step == 0)
    def _():
        copies = [
            pltpu.make_async_copy(src, dst, sem.at[at])
            for at, (src, dst) in enumerate(
                (
                    (q1, q1_s),
                    (q2, q2_s),
                    (q3, q3_s),
                    (kv1, kv1_s),
                    (kv2, kv2_s),
                    (kv3, kv3_s),
                    (tokens, tok_s),
                    (near, near_s),
                    (qk0, qk0_s),
                    (vt0, vt0_s),
                    (stats, stats_s),
                )
            )
        ]
        for copy in copies:
            copy.start()
        for p in range(4):
            wso_s[p * 256 : p * 256 + GW, :] = weights(p)
            wso_s[p * 256 + GW : (p + 1) * 256, :] = jnp.zeros((64, SW), BF16)
        embed_out[...] = em[pl.ds(pl.multiple_of((place // 8) * 8, 8), 8), :][0:3].astype(BF16)
        far_s[...] = jnp.zeros_like(far_s)
        for copy in copies:
            copy.wait()

        def put(ref, row, vector, columns=None):
            base = pl.multiple_of((row // 16) * 16, 16)
            width = ref.shape[1]
            block = ref[pl.ds(base, 16), :].astype(F32)
            hit = lax.broadcasted_iota(jnp.int32, (16, width), 0) == row - base
            if columns is not None:
                hit = jnp.logical_and(hit, columns)
            ref[pl.ds(base, 16), :] = jnp.where(hit, vector, block).astype(BF16)

        head16 = head_of((16, 384))

        def insert(n, found):
            pos = positions[n]
            owner = jnp.right_shift(pos, 11)
            here = jnp.bitwise_and(pos, ROWS - 1)
            local = owner == place

            @pl.when(local)
            def _():
                put(tok_s, here, em[pl.ds((n // 3) * 8 + n % 3, 1), :])

            for p, q_s, kv_s in ((1, q1_s, kv1_s), (2, q2_s, kv2_s), (3, q3_s, kv3_s)):
                bits = (0, 3, 5, 7)[p]
                member = jnp.bitwise_and(pos, DIL[p] - 1)
                within = jnp.right_shift(owner, bits) == jnp.right_shift(place, bits)
                at = jnp.right_shift(here, bits)

                @pl.when(jnp.logical_and(member < 4, within))
                def _():
                    if p == 1:
                        slot = jnp.bitwise_and(owner, 7)
                    else:
                        grp = jnp.right_shift(owner, 3)
                        of_core = jnp.right_shift(grp, 1) * 8 + jnp.bitwise_and(owner, 7)
                        many = (0, 8, 16, 64)[p]
                        slot = jnp.bitwise_and(grp, 1) * many + jnp.bitwise_and(of_core, many - 1)
                    columns = head16 == member
                    put(
                        kv_s,
                        slot * (ROWS // DIL[p]) + at,
                        new[pl.ds(n, 1), p * SW : p * SW + 384],
                        columns,
                    )

                    @pl.when(local)
                    def _():
                        put(q_s, at, new[pl.ds(n, 1), p * SW + 384 : (p + 1) * SW], columns)

            return found + jnp.where(local, 1, 0)

        found = lax.fori_loop(0, 48, insert, jnp.int32(0))

        @pl.when(jnp.min(stats_s[4:8]) < 2.0**-60)
        def _():
            @pl.loop(0, 16)
            def _(u):
                j = u % 4
                at = pl.ds(pl.multiple_of(u // 4 * 512, 512), 512)
                q = qk0_s[at, 0:256]
                s = dot_nt(
                    qk0_s[:, 256:512], jnp.where(only_head(j, 512, True), q, jnp.zeros_like(q))
                )
                m = jnp.max(s, axis=0, keepdims=True)
                e = jnp.exp2((s - m) * SCALE).astype(BF16)
                o = dot(vt0_s[pl.ds(pl.multiple_of(j * 64, 64), 64), :], e)
                count = o[SH : SH + 1, :]
                rows = pl.ds(pl.multiple_of(j * SH, 16), SH)
                near_s[rows, at] = (o[:SH, :] / count).astype(BF16)
                stats_s[j, :, at] = jnp.broadcast_to(m, (8, 512))
                stats_s[4 + j, :, at] = jnp.broadcast_to(count, (8, 512))

        @pl.when(found > 0)
        def _():
            slots = lax.broadcasted_iota(jnp.int32, (48, 1), 0)
            places = lax.fori_loop(
                0,
                48,
                lambda n, held: jnp.where(slots == n, positions[n], held),
                jnp.full((48, 1), -1, jnp.int32),
            )
            hide = jnp.where(places // ROWS == place, 0.0, HIDE)
            lane = lax.broadcasted_iota(jnp.int32, (48, 256), 1)
            fresh_q = jnp.where(lane == GW, 1.0, new[:, 0:256]).astype(BF16)
            fresh_k = new[:, 256:512].astype(BF16)
            fresh_vt = with_ones(new[:, 512 : 512 + GW].T)

            made = []
            for j in range(4):
                q = jnp.where(only_head(j, 48, True), fresh_q, jnp.zeros_like(fresh_q))
                s_old = dot_nt(qk0_s[:, 256:512], q)
                s_new = dot_nt(fresh_k, q) + hide
                m = jnp.maximum(
                    jnp.max(s_old, axis=0, keepdims=True), jnp.max(s_new, axis=0, keepdims=True)
                )
                e_old = jnp.exp2((s_old - m) * SCALE).astype(BF16)
                e_new = jnp.exp2((s_new - m) * SCALE).astype(BF16)
                head_rows = slice(j * 64, (j + 1) * 64)
                o = dot(vt0_s[head_rows, :], e_old) + dot(fresh_vt[head_rows, :], e_new)
                made.append(o[:SH, :] / o[SH : SH + 1, :])
            made = jnp.concatenate(made, axis=0).astype(BF16)

            @pl.loop(0, 4)
            def _(b):
                at = pl.ds(pl.multiple_of(b * 512, 512), 512)
                q = qk0_s[at, 0:256]
                joined = []
                for j in range(4):
                    k = jnp.where(only_head(j, 48, False), fresh_k, jnp.zeros_like(fresh_k))
                    s = dot_nt(k, q) + hide
                    m_old = stats_s[j, 0:1, at]
                    m = jnp.maximum(m_old, jnp.max(s, axis=0, keepdims=True))
                    weight = stats_s[4 + j, 0:1, at] * jnp.exp2((m_old - m) * SCALE)
                    e = jnp.exp2((s - m) * SCALE).astype(BF16)
                    o = dot(fresh_vt[j * 64 : (j + 1) * 64, :], e)
                    held = near_s[j * SH : (j + 1) * SH, at].astype(F32)
                    joined.append((held * weight + o[:SH, :]) / (weight + o[SH : SH + 1, :]))
                row = lax.broadcasted_iota(jnp.int32, (48, 512), 1) + (place * ROWS + b * 512)
                hit = jnp.where(row == places, 1.0, 0.0)
                anew = dot(made, hit.astype(BF16))
                taken = jnp.max(hit, axis=0, keepdims=True) > 0.0
                near_s[:, at] = jnp.where(taken, anew, jnp.concatenate(joined, axis=0)).astype(
                    BF16
                )

        def far_heads(p, q_s, kv_s, heads):
            r = DIL[p]
            count = ROWS // r
            q = q_s[...]
            kv = kv_s[...]
            head = head_of((count, 384))
            stack = [jnp.where(head == j, q, jnp.zeros_like(q)) for j in heads]
            _, e, o = attend(jnp.concatenate(stack, axis=0), kv, kv)
            o = o[:, 0:256] / jnp.sum(e.astype(F32), axis=-1, keepdims=True)
            for at, j in enumerate(heads):
                mine = jnp.where(
                    only_head(j, count, False), o[at * count : (at + 1) * count, :], 0.0
                )
                for b in range(2):
                    far_s[2 * (p - 1) + b, pl.ds(j, count, stride=r), :] = mine[
                        :, b * 128 : (b + 1) * 128
                    ]

        for j in range(4):
            far_heads(1, q1_s, kv1_s, (j,))
        far_heads(2, q2_s, kv2_s, (0, 1, 2, 3))
        far_heads(3, q3_s, kv3_s, (0, 1, 2, 3))

    at = pl.ds(pl.multiple_of(step * 512, 512), 512)

    near_t = jnp.concatenate([near_s[:, at], jnp.zeros((64, 512), BF16)], axis=0).T
    far = jnp.concatenate([far_s[b, at, :] for b in range(6)], axis=1).astype(BF16)
    total = tok_s[at, :].astype(F32) + dot(jnp.concatenate([near_t, far], axis=1), wso_s[...])
    out[...] = total.astype(BF16)


def run_slide(*args):
    hbm = pl.BlockSpec(memory_space=pl.ANY)
    vmem = pl.BlockSpec(memory_space=pltpu.VMEM)
    return pl.pallas_call(
        slide_kernel,
        out_shape=(
            jax.ShapeDtypeStruct((ROWS, SW), BF16),
            jax.ShapeDtypeStruct((3, SW), BF16),
        ),
        grid_spec=pltpu.PrefetchScalarGridSpec(
            num_scalar_prefetch=2,
            grid=(4,),
            in_specs=[hbm] * 11 + [vmem] * 3,
            out_specs=(
                pl.BlockSpec((512, SW), lambda i, *_: (i, 0)),
                pl.BlockSpec((3, SW), lambda i, *_: (0, 0)),
            ),
            scratch_shapes=[
                pltpu.VMEM((ROWS, 512), BF16),
                pltpu.VMEM((256, ROWS), BF16),
                pltpu.VMEM((GW, ROWS), BF16),
                pltpu.VMEM((8, 8, ROWS), F32),
                pltpu.VMEM((256, 384), BF16),
                pltpu.VMEM((64, 384), BF16),
                pltpu.VMEM((16, 384), BF16),
                pltpu.VMEM((2048, 384), BF16),
                pltpu.VMEM((2048, 384), BF16),
                pltpu.VMEM((2048, 384), BF16),
                pltpu.VMEM((ROWS, SW), BF16),
                pltpu.VMEM((6, ROWS, 128), F32),
                pltpu.VMEM((1024, SW), BF16),
                pltpu.SemaphoreType.DMA((11,)),
            ],
        ),
        compiler_params=pltpu.CompilerParams(vmem_limit_bytes=56 * 1024 * 1024),
        name="slide",
    )(*args)


def shards(
    tile_patches,
    w_patch,
    w_tqkv,
    w_to,
    w_gu,
    w_down,
    tile_gain,
    w_in,
    slide_tokens,
    slide_gain,
    w_sqkv,
    w_so,
    pattern_of_group,
    new_positions,
):
    qk0, vt0, near, stats, q1, q2, q3, kv1, kv2, kv3, em, new = run_encoder(
        tile_patches,
        w_patch,
        jnp.transpose(w_tqkv, (0, 2, 1)),
        w_to,
        w_gu,
        w_down,
        w_in,
        slide_tokens,
        w_sqkv,
        tile_gain,
        slide_gain,
        new_positions,
        pattern_of_group,
    )
    slide_out, tile_embed = run_slide(
        new_positions,
        pattern_of_group,
        qk0,
        vt0,
        near,
        stats,
        q1,
        q2,
        q3,
        kv1,
        kv2,
        kv3,
        slide_tokens,
        new,
        em.reshape(128, SW),
        w_so,
    )
    return (tile_embed, slide_out)


def solution(mesh):
    placed = (
        P(("grp", "dev"), None),
        P(),
        P(None, None, "dev"),
        P("dev", None),
        P(None, None, "dev"),
        P("dev", None),
        P(),
        P(),
        P(("grp", "dev"), None),
        P(),
        P(),
        P(),
        P(),
        P(),
    )
    return jax.shard_map(
        shards,
        mesh=mesh,
        in_specs=placed,
        out_specs=(P("grp", None), P(("grp", "dev"), None)),
        check_vma=False,
    )
```

profile of v0, /device:TPU:8, one launch (start us, length us, event | category | flops | bytes accessed | tf_op | source)
XLA Modules:
  0.0 148.7 jit_solution(14235441020740714236)
XLA Ops:
  0.6 89.3 %encode.1 = (bf16[2048,512]{1,0:T(8,128)(2,1)}, bf16[256,2048]{1,0:T(8,128)(2,1)}, bf16[192,2048]{1,0:T(8,128)(2,1)}, f32[8,8,2048]{2,1,0:T(8,128)}, bf16[256,38...) custom-call(bf16[96,588]{1,0:T(8,128)(2,1)} %patches.1, ...), custom_call_target="tpu_custom_call" | custom-call | tf_op jit(solution)/shard_map/encode/pallas_call | solution.py:513
  89.9 58.7 %slide.1 = (bf16[2048,768]{1,0:T(8,128)(2,1)}, bf16[3,768]{1,0:T(4,128)(2,1)}) custom-call(s32[48]{0:T(128)} %positions.3, s32[4]{0:T(128)} %pattern.3, bf16[2048,512]{1,0:T(8,128)(2,1)} %get-tuple-element.16.qk0, bf16[256,2048]{1,0:T(8,128)(2,1)} %get-tuple-element.17.vt0, bf16[192,2048]{1,0:T(8,128)(2,1)} %get-tuple-element.18.near, ...), custom_call_target="tpu_custom_call" | custom-call | tf_op jit(solution)/shard_map/slide/pallas_call | solution.py:797
where the time goes:
time: 149 us
  Pallas kernels  148 us (99%)
    pallas_call x1, Pallas kernels, run_encoder(): pl.pallas_call(encoder_kernel, out_shape=(shape((ROWS, 512), BF16), shape...  89.3 us
    pallas_call x1, Pallas kernels, run_slide(): pl.pallas_call(slide_kernel, out_shape=(jax.ShapeDtypeStruct((ROWS, SW),...  58.7 us

commit v1 on v0

--- a/solution.py
+++ b/solution.py
@@ -23,7 +23,7 @@
 DIL = (1, 8, 32, 128)
 LOG2E = 1.4426950408889634
 HIDE = -1e30
-KEYS_AT, HALF_AT, FEED_AT, EMBED_AT = 6, 10, 12, 14
+KEYS_AT, HALF_AT, FEED_AT, EMBED_AT = 9, 8, 12, 14
 SCALE = LOG2E * SH**-0.5
 
 
@@ -206,11 +206,11 @@
 
     @pl.loop(1, 8)
     def _(i):
-        push(patches, patches_s.at[my_patch], 0, peer8(i))
+        push(w_to.at[pl.ds(half_row, 96), quarter], wto_s.at[my_half, quarter], 1, peer8(i))
 
     @pl.loop(1, 8)
     def _(i):
-        push(w_to.at[pl.ds(half_row, 96), quarter], wto_s.at[my_half, quarter], 1, peer8(i))
+        push(patches, patches_s.at[my_patch], 0, peer8(i))
 
     ld_raw.wait()
     group = [
@@ -270,6 +270,17 @@
         qk0_s[at, 256:512] = jnp.where(column == GW, stale * HIDE, k.astype(F32)).astype(BF16)
         vt0_s[:, at] = with_ones(y[:, 512 : 512 + GW].T)
 
+    own_wto.wait()
+    landed(wto_s.at[pl.ds(0, 672), quarter], recv_sem.at[1])
+
+    @pl.loop(1, 8)
+    def _(i):
+        half = pl.ds(pl.multiple_of(((dev + i) % 8) * HB + core * 96, 32), 96)
+
+        @pl.loop(1, 4)
+        def _(step):
+            push(wto_s.at[half, quarter], wto_s.at[half, quarter], 10, peer_x(step))
+
     bound = (jnp.sqrt(largest[...]) * 1.02).astype(BF16)
 
     @pl.loop(0, 8)
@@ -293,19 +304,6 @@
     @pl.loop(0, 3)
     def _(t):
         at = pl.ds(pl.multiple_of(t * TP, TP), TP)
-        @pl.when(t == 1)
-        def _():
-            own_wto.wait()
-            landed(wto_s.at[pl.ds(0, 672), quarter], recv_sem.at[1])
-
-            @pl.loop(1, 8)
-            def _(i):
-                half = pl.ds(pl.multiple_of(((dev + i) % 8) * HB + core * 96, 32), 96)
-
-                @pl.loop(1, 4)
-                def _(step):
-                    push(wto_s.at[half, quarter], wto_s.at[half, quarter], 10, peer_x(step))
-
         x0 = dot(patches_s[at, :], w_patch_s[...]).astype(BF16)
         x0_s[at, :] = x0
         h1 = norm(x0.astype(F32), tgain[0:1, :]).astype(BF16)
@@ -633,7 +631,7 @@
             wso_s[p * 256 + GW : (p + 1) * 256, :] = jnp.zeros((64, SW), BF16)
         embed_out[...] = em[pl.ds(pl.multiple_of((place // 8) * 8, 8), 8), :][0:3].astype(BF16)
         far_s[...] = jnp.zeros_like(far_s)
-        for copy in copies:
+        for copy in copies[:7]:
             copy.wait()
 
         def put(ref, row, vector, columns=None):
@@ -687,6 +685,9 @@
             return found + jnp.where(local, 1, 0)
 
         found = lax.fori_loop(0, 48, insert, jnp.int32(0))
+
+        for copy in copies[7:]:
+            copy.wait()
 
         @pl.when(jnp.min(stats_s[4:8]) < 2.0**-60)
         def _():
@@ -710,41 +711,60 @@
         @pl.when(found > 0)
         def _():
             slots = lax.broadcasted_iota(jnp.int32, (48, 1), 0)
-            places = lax.fori_loop(
+            lanes = lax.broadcasted_iota(jnp.int32, (1, 48), 1)
+            nowhere = (jnp.full((48, 1), -1, jnp.int32), jnp.full((1, 48), -1, jnp.int32))
+            places, across = lax.fori_loop(
                 0,
                 48,
-                lambda n, held: jnp.where(slots == n, positions[n], held),
-                jnp.full((48, 1), -1, jnp.int32),
+                lambda n, held: (
+                    jnp.where(slots == n, positions[n], held[0]),
+                    jnp.where(lanes == n, positions[n], held[1]),
+                ),
+                nowhere,
             )
-            hide = jnp.where(places // ROWS == place, 0.0, HIDE)
+            hide = jnp.where(jnp.right_shift(places, 11) == place, 0.0, HIDE)
+            hide = jnp.concatenate([hide] * 4, axis=0)
+            hide_across = jnp.where(jnp.right_shift(across, 11) == place, 0.0, HIDE)
             lane = lax.broadcasted_iota(jnp.int32, (48, 256), 1)
             fresh_q = jnp.where(lane == GW, 1.0, new[:, 0:256]).astype(BF16)
             fresh_k = new[:, 256:512].astype(BF16)
             fresh_vt = with_ones(new[:, 512 : 512 + GW].T)
 
+            def stacked(rows, bias):
+                return jnp.concatenate(
+                    [
+                        jnp.where(only_head(j, 48, bias), rows, jnp.zeros_like(rows))
+                        for j in range(4)
+                    ],
+                    axis=0,
+                )
+
+            q = stacked(fresh_q, True)
+            s_old = dot_nt(q, qk0_s[:, 256:512])
+            s_new = dot_nt(q, fresh_k) + hide_across
+            m = jnp.maximum(
+                jnp.max(s_old, axis=1, keepdims=True), jnp.max(s_new, axis=1, keepdims=True)
+            )
+            e_old = jnp.exp2((s_old - m) * SCALE).astype(BF16)
+            e_new = jnp.exp2((s_new - m) * SCALE).astype(BF16)
             made = []
             for j in range(4):
-                q = jnp.where(only_head(j, 48, True), fresh_q, jnp.zeros_like(fresh_q))
-                s_old = dot_nt(qk0_s[:, 256:512], q)
-                s_new = dot_nt(fresh_k, q) + hide
-                m = jnp.maximum(
-                    jnp.max(s_old, axis=0, keepdims=True), jnp.max(s_new, axis=0, keepdims=True)
+                head_rows = slice(j * 64, (j + 1) * 64)
+                of_head = slice(j * 48, (j + 1) * 48)
+                o = dot_nt(vt0_s[head_rows, :], e_old[of_head]) + dot_nt(
+                    fresh_vt[head_rows, :], e_new[of_head]
                 )
-                e_old = jnp.exp2((s_old - m) * SCALE).astype(BF16)
-                e_new = jnp.exp2((s_new - m) * SCALE).astype(BF16)
-                head_rows = slice(j * 64, (j + 1) * 64)
-                o = dot(vt0_s[head_rows, :], e_old) + dot(fresh_vt[head_rows, :], e_new)
                 made.append(o[:SH, :] / o[SH : SH + 1, :])
             made = jnp.concatenate(made, axis=0).astype(BF16)
+            k = stacked(fresh_k, False)
 
             @pl.loop(0, 4)
             def _(b):
                 at = pl.ds(pl.multiple_of(b * 512, 512), 512)
-                q = qk0_s[at, 0:256]
+                all_s = dot_nt(k, qk0_s[at, 0:256]) + hide
                 joined = []
                 for j in range(4):
-                    k = jnp.where(only_head(j, 48, False), fresh_k, jnp.zeros_like(fresh_k))
-                    s = dot_nt(k, q) + hide
+                    s = all_s[j * 48 : (j + 1) * 48, :]
                     m_old = stats_s[j, 0:1, at]
                     m = jnp.maximum(m_old, jnp.max(s, axis=0, keepdims=True))
                     weight = stats_s[4 + j, 0:1, at] * jnp.exp2((m_old - m) * SCALE)

time: 149 us -> 147 us (0.987)
  the two profiles are of different devices: /device:TPU:8 before, /device:TPU:1 now
where the time goes in v1:
time: 147 us
  Pallas kernels  146 us (99%)
    pallas_call x1, Pallas kernels, run_encoder(): pl.pallas_call(encoder_kernel, out_shape=(shape((ROWS, 512), BF16), shape...  94.5 us
    pallas_call x1, Pallas kernels, run_slide(): pl.pallas_call(slide_kernel, out_shape=(jax.ShapeDtypeStruct((ROWS, SW),...  52 us

profile of v1, /device:TPU:1, one launch (start us, length us, event | category | flops | bytes accessed | tf_op | source)
XLA Modules:
  0.0 147.3 jit_solution(5637896657595452899)
XLA Ops:
  0.6 94.5 %encode.1 = (bf16[2048,512]{1,0:T(8,128)(2,1)}, bf16[256,2048]{1,0:T(8,128)(2,1)}, bf16[192,2048]{1,0:T(8,128)(2,1)}, f32[8,8,2048]{2,1,0:T(8,128)}, bf16[256,38...) custom-call(bf16[96,588]{1,0:T(8,128)(2,1)} %patches.1, ...), custom_call_target="tpu_custom_call" | custom-call | tf_op jit(solution)/shard_map/encode/pallas_call | solution.py:511
  95.1 52.0 %slide.1 = (bf16[2048,768]{1,0:T(8,128)(2,1)}, bf16[3,768]{1,0:T(4,128)(2,1)}) custom-call(s32[48]{0:T(128)} %positions.3, s32[4]{0:T(128)} %pattern.3, bf16[2048,512]{1,0:T(8,128)(2,1)} %get-tuple-element.16.qk0, bf16[256,2048]{1,0:T(8,128)(2,1)} %get-tuple-element.17.vt0, bf16[192,2048]{1,0:T(8,128)(2,1)} %get-tuple-element.18.near, ...), custom_call_target="tpu_custom_call" | custom-call | tf_op jit(solution)/shard_map/slide/pallas_call | solution.py:817

commit v2 on v1

--- a/solution.py
+++ b/solution.py
@@ -23,7 +23,7 @@
 DIL = (1, 8, 32, 128)
 LOG2E = 1.4426950408889634
 HIDE = -1e30
-KEYS_AT, HALF_AT, FEED_AT, EMBED_AT = 9, 8, 12, 14
+KEYS_AT, HALF_AT, FEED_AT, EMBED_AT = 3, 11, 12, 14
 SCALE = LOG2E * SH**-0.5
 
 
@@ -206,10 +206,6 @@
 
     @pl.loop(1, 8)
     def _(i):
-        push(w_to.at[pl.ds(half_row, 96), quarter], wto_s.at[my_half, quarter], 1, peer8(i))
-
-    @pl.loop(1, 8)
-    def _(i):
         push(patches, patches_s.at[my_patch], 0, peer8(i))
 
     ld_raw.wait()
@@ -270,17 +266,6 @@
         qk0_s[at, 256:512] = jnp.where(column == GW, stale * HIDE, k.astype(F32)).astype(BF16)
         vt0_s[:, at] = with_ones(y[:, 512 : 512 + GW].T)
 
-    own_wto.wait()
-    landed(wto_s.at[pl.ds(0, 672), quarter], recv_sem.at[1])
-
-    @pl.loop(1, 8)
-    def _(i):
-        half = pl.ds(pl.multiple_of(((dev + i) % 8) * HB + core * 96, 32), 96)
-
-        @pl.loop(1, 4)
-        def _(step):
-            push(wto_s.at[half, quarter], wto_s.at[half, quarter], 10, peer_x(step))
-
     bound = (jnp.sqrt(largest[...]) * 1.02).astype(BF16)
 
     @pl.loop(0, 8)
@@ -296,6 +281,10 @@
 
     own_patch.wait()
     landed(patches_s.at[pl.ds(0, 672)], recv_sem.at[0])
+    @pl.loop(1, 8)
+    def _(i):
+        push(w_to.at[pl.ds(half_row, 96), quarter], wto_s.at[my_half, quarter], 1, peer8(i))
+
     ld_patch.wait()
     ld_tqkv.wait()
 
@@ -328,6 +317,17 @@
                 device_id=peer8(i),
                 device_id_type=MESH,
             ).start()
+
+    own_wto.wait()
+    landed(wto_s.at[pl.ds(0, 672), quarter], recv_sem.at[1])
+
+    @pl.loop(1, 8)
+    def _(i):
+        half = pl.ds(pl.multiple_of(((dev + i) % 8) * HB + core * 96, 32), 96)
+
+        @pl.loop(1, 4)
+        def _(step):
+            push(wto_s.at[half, quarter], wto_s.at[half, quarter], 10, peer_x(step))
 
     for p, kvc, q_out in ((1, kvc1, q1_out), (2, kvc2, q2_out), (3, kvc3, q3_out)):
         r = DIL[p]
@@ -401,7 +401,6 @@
             def _(i):
                 push(kvc3, kv3.at[at3], 2, peer_z(i))
                 push(kvc2, kv2.at[at2], 11, peer_z(i))
-                push(kvc1, kv1.at[at1], 14, peer_z(i))
 
         @pl.when(u == HALF_AT)
         def _():
@@ -424,6 +423,7 @@
             def _(i):
                 push(kv3.at[at3_z], kv3.at[at3_z], 3, peer_y(i))
                 push(kv2.at[at2_z], kv2.at[at2_z], 12, peer_y(i))
+                push(kvc1, kv1.at[at1], 14, peer_z(i))
                 push(kv1.at[at1_y], kv1.at[at1_y], 14, peer_z(i))
 
             landed(wto_s.at[pl.ds(0, 672)], recv_sem.at[5])

time: 147 us -> 146 us (level); the launches traced: 147 us -> 143 us
  Pallas kernels: 146 us -> 142 us
    pallas_call x1, Pallas kernels: 52 us -> 48.5 us  [run_slide(): pl.pallas_call(slide_kernel, out_shape=(jax.ShapeDtypeStruct((ROWS, SW),...]
where the time goes in v2:
time: 146 us; the launch traced here: 143 us
  Pallas kernels  142 us (97%)
    pallas_call x1, Pallas kernels, run_encoder(): pl.pallas_call(encoder_kernel, out_shape=(shape((ROWS, 512), BF16), shape...  93.9 us
    pallas_call x1, Pallas kernels, run_slide(): pl.pallas_call(slide_kernel, out_shape=(jax.ShapeDtypeStruct((ROWS, SW),...  48.5 us

profile of v2, /device:TPU:1, one launch (start us, length us, event | category | flops | bytes accessed | tf_op | source)
XLA Modules:
  0.0 143.2 jit_solution(12201892221188214084)
XLA Ops:
  0.6 93.9 %encode.1 = (bf16[2048,512]{1,0:T(8,128)(2,1)}, bf16[256,2048]{1,0:T(8,128)(2,1)}, bf16[192,2048]{1,0:T(8,128)(2,1)}, f32[8,8,2048]{2,1,0:T(8,128)}, bf16[256,38...) custom-call(bf16[96,588]{1,0:T(8,128)(2,1)} %patches.1, ...), custom_call_target="tpu_custom_call" | custom-call | tf_op jit(solution)/shard_map/encode/pallas_call | solution.py:511
  94.6 48.5 %slide.1 = (bf16[2048,768]{1,0:T(8,128)(2,1)}, bf16[3,768]{1,0:T(4,128)(2,1)}) custom-call(s32[48]{0:T(128)} %positions.3, s32[4]{0:T(128)} %pattern.3, bf16[2048,512]{1,0:T(8,128)(2,1)} %get-tuple-element.16.qk0, bf16[256,2048]{1,0:T(8,128)(2,1)} %get-tuple-element.17.vt0, bf16[192,2048]{1,0:T(8,128)(2,1)} %get-tuple-element.18.near, ...), custom_call_target="tpu_custom_call" | custom-call | tf_op jit(solution)/shard_map/slide/pallas_call | solution.py:817
